TPU v7x, 128 devices: a whole 4x4x4 slice. The times are simulated.
128 devices in a mesh: vid: 8 (over x, core), fsdp: 16 (over y, z).
Axes of the slice: x: 4, y: 4, z: 4, core: 2. Of those that a mesh axis runs over, the one named last changes fastest.
Arguments:
- latents: bfloat16 [64, 256, 6144], P('vid', 'fsdp'), may hold values from -6 to 6
- shift_mod: float32 [64, 6144], P('vid'), may hold values from -3 to 3
- scale_mod: float32 [64, 6144], P('vid'), may hold values from -3 to 3
- qkv_weight: bfloat16 [6144, 3, 4096], P(None, None, 'fsdp'), may hold values from -0.078125 to 0.078125
- kv_cache: bfloat16 [64, 4, 2, 256, 4096], P('vid', None, None, None, 'fsdp'), may hold values from -6 to 6
- holders: int32 [64], replicated, may hold values from 0 to 63, as said below
- cached: int32 [64], replicated, may hold values from 1 to 4
Outputs:
- attended: bfloat16 [64, 256, 4096], P('vid', None, 'fsdp')
Inputs may be any that keep to these rules, and one draw needn't show every extreme that they name: holders is a permutation of the 64 cache slots. Slot s lies on index s // 8 of vid; the owner of video v is index v // 8 of vid. Each index of vid holds exactly one video of each owner.
All inputs are finite; a program needn't handle non-finite values.
Results may differ from a plain program's by a relative error of at most 0.0048.
Values may be sent and summed in bfloat16 or wider, within the bound.
No kernel may reach another device: no remote copies, remote signals or barrier semaphores. Data moves between devices by JAX's collectives and lax.ppermute only.
A program may use at most 192 MiB of HBM per device.

v0:
```python
import math

import jax
import jax.numpy as jnp
from jax import lax
from jax.sharding import PartitionSpec as P

HEAD = 128
GROUP_TOKENS = 256
MAXC = 4


def rms_scale(values):
    return values * lax.rsqrt(jnp.mean(values * values, axis=-1, keepdims=True) + 1e-06)


def modulate(latent_rows, shift_rows, scale_rows):
    widened = latent_rows.astype(jnp.float32)
    center = jnp.mean(widened, axis=-1, keepdims=True)
    offsets = widened - center
    spread = jnp.mean(offsets * offsets, axis=-1, keepdims=True)
    return (offsets * lax.rsqrt(spread + 1e-06) * (1.0 + scale_rows) + shift_rows).astype(
        jnp.bfloat16
    )


def attend_group_block(query_rows, group_key_rows, group_value_rows, active_flags):
    logit_scores = jnp.einsum(
        "vqhd,vkhd->vhqk", query_rows, group_key_rows, preferred_element_type=jnp.float32
    ) / math.sqrt(HEAD)
    softmax_weights = jnp.exp(logit_scores)
    if active_flags is not None:
        softmax_weights = softmax_weights * active_flags[:, None, None, :]
    totals = jnp.transpose(jnp.sum(softmax_weights, axis=-1), (0, 2, 1))
    summed = jnp.einsum(
        "vhqk,vkhd->vqhd",
        softmax_weights.astype(jnp.bfloat16),
        group_value_rows,
        preferred_element_type=jnp.float32,
    )
    return (summed, totals)


def split_cache(blocks, heads_here):
    count_rows = blocks.shape[0]
    previous_keys = rms_scale(
        blocks[:, :, 0]
        .astype(jnp.float32)
        .reshape(count_rows, MAXC * GROUP_TOKENS, heads_here, HEAD)
    ).astype(jnp.bfloat16)
    previous_values = blocks[:, :, 1].reshape(count_rows, MAXC * GROUP_TOKENS, heads_here, HEAD)
    return (previous_keys, previous_values)


def invert(places, length):
    identities = jnp.arange(length, dtype=jnp.int32)
    return jnp.sum(
        (places[None, :] == identities[:, None]).astype(jnp.int32) * identities[None, :], axis=1
    )


def shards(latents, shift_mod, scale_mod, qkv_weight, kv_cache, holders, cached):
    vid_total = lax.axis_size("vid")
    vid_place = lax.axis_index("vid")
    per_device = latents.shape[0]
    per_owner = per_device // vid_total
    model_width = qkv_weight.shape[0]
    local_width = qkv_weight.shape[2]
    heads_here = local_width // HEAD
    normed = modulate(latents, shift_mod[:, None, :], scale_mod[:, None, :])
    weight_matrix = qkv_weight.reshape(model_width, 3 * local_width)
    rows_piece = lax.all_gather(normed, "fsdp", axis=1, tiled=True)
    projected = jnp.einsum(
        "vtd,dk->vtk", rows_piece, weight_matrix, preferred_element_type=jnp.float32
    )
    projected = projected.reshape(rows_piece.shape[0], rows_piece.shape[1], 3, heads_here, HEAD)
    packed = jnp.stack(
        [rms_scale(projected[:, :, 0]), rms_scale(projected[:, :, 1]), projected[:, :, 2]], axis=2
    ).astype(jnp.bfloat16)
    query_rows = packed[:, :, 0]
    current_sum, current_total = attend_group_block(
        query_rows, packed[:, :, 1], packed[:, :, 2], None
    )
    slot_count = holders.shape[0]
    slot_ids = jnp.arange(slot_count, dtype=jnp.int32)
    matches = (holders[None, :] == slot_ids[:, None]).astype(jnp.int32)
    video_at = jnp.sum(matches * slot_ids[None, :], axis=1)
    owner_at = video_at // per_device
    holder_at = slot_ids // per_device
    earlier = (
        (holder_at[:, None] == holder_at[None, :])
        & (owner_at[:, None] == owner_at[None, :])
        & (slot_ids[None, :] < slot_ids[:, None])
    )
    rank_at = jnp.sum(earlier.astype(jnp.int32), axis=1)
    first_row = vid_place * per_device
    slot_places = lax.dynamic_slice_in_dim(owner_at * per_owner + rank_at, first_row, per_device)
    slot_order = invert(slot_places, per_device)
    video_slots = lax.dynamic_slice_in_dim(holders, first_row, per_device)
    video_places = video_slots // per_device * per_owner + jnp.take(rank_at, video_slots)
    group_position_index = jnp.arange(MAXC * GROUP_TOKENS, dtype=jnp.int32) // GROUP_TOKENS
    arrived = lax.all_to_all(
        jnp.take(kv_cache, slot_order, axis=0), "vid", split_axis=0, concat_axis=0, tiled=True
    )
    received_blocks = jnp.take(arrived, video_places, axis=0)
    previous_keys, previous_values = split_cache(received_blocks, heads_here)
    video_active = lax.dynamic_slice_in_dim(cached, first_row, per_device)
    active_flags = (group_position_index[None, :] < video_active[:, None]).astype(jnp.float32)
    previous_sum, previous_total = attend_group_block(
        query_rows, previous_keys, previous_values, active_flags
    )
    blended = (current_sum + previous_sum) / (current_total + previous_total)[:, :, :, None]
    return blended.astype(jnp.bfloat16).reshape(per_device, blended.shape[1], local_width)


def solution(mesh):
    return jax.shard_map(
        shards,
        mesh=mesh,
        in_specs=(
            P("vid", "fsdp", None),
            P("vid", None),
            P("vid", None),
            P(None, None, "fsdp"),
            P("vid", None, None, None, "fsdp"),
            P(),
            P(),
        ),
        out_specs=P("vid", None, "fsdp"),
        check_vma=False,
    )
```

profile of v0, /device:TPU:4, one launch (start us, length us, event | category | flops | bytes accessed | tf_op | source)
XLA Modules:
  0.0 254.7 jit_solution(2960442737859261844)
XLA Ops:
  6.5 0.0 copy-start.1
  6.5 0.0 all-gather.2.cloned.1.call-start
  6.5 1.1 broadcast_add_fusion
  7.6 0.0 copy-start.2
  7.6 1.7 convert_reduce_fusion
  9.3 2.0 fusion.15
  11.3 0.0 copy-done.1
  11.3 2.9 %fusion.18 = bf16[8,16,6144]{2,1,0:T(8,128)(2,1)} fusion(bf16[8,16,6144]{2,1,0:T(8,128)(2,1)S(1)} %copy-done.1, f32[8,6144]{1,0:T(8,128)} %param.10, f32[8,6144]{1,0:T(8,128)S(1)} %broadcast_add_fusion, f32[8,16]{1,0:T(8,128)S(1)} %add_rsqrt_fusion.3, f32[8,16]{1,0:T(8,128)S(1)} %broadcast_multiply_fusion), kind=kLoop, calls=%fused_computation.29 | loop fusion | flops 4718592 | bytes 3539968 | tf_op jit(solution)/shard_map/convert_element_type | solution.py:22
  14.2 0.0 all-gather.2.cloned.1.call-update
  14.2 0.0 copy-done.2
  14.2 0.1 select_reduce_fusion
  14.4 0.2 convert_reduce_fusion.1
  14.6 0.1 dynamic_slice.9
  14.6 0.1 select_reduce_fusion.1
  14.8 8.1 %gather_fusion.1 = bf16[8,4,2,256,256]{4,3,2,1,0:T(8,128)(2,1)} fusion(bf16[8,4,2,256,256]{4,3,2,1,0:T(8,128)(2,1)} %param.13, s32[1024]{0:T(1024)S(1)} %pad_clamp_fusion.1), kind=kCustom, calls=%fused_computation.clone | custom fusion | bytes 16777248 | tf_op jit(solution)/shard_map/jit(_take)/gather | solution.py:103
  22.9 8.0 %broadcast_select_fusion.1 = bf16[8,4,2,256,256]{4,3,2,1,0:T(8,128)(2,1)} fusion(bf16[8,4,2,256,256]{4,3,2,1,0:T(8,128)(2,1)} %gather_fusion.1, pred[8]{0:T(512)(128)(4,1)S(1)} %compare_and_fusion.1), kind=kLoop, calls=%fused_computation.14 | loop fusion | flops 4194304 | bytes 16777224 | tf_op jit(solution)/shard_map/jit(_take)/select_n | solution.py:103
  30.9 5.2 %all-to-all-start = ((bf16[8,4,2,256,256]{4,3,2,1,0:T(8,128)(2,1)}), bf16[8,4,2,256,256]{4,3,2,1,0:T(8,128)(2,1)}, u32[]{:S(2)}, u32[]{:S(2)}) async-start(bf16[8,4,2,256,256]{4,3,2,1,0:T(8,128)(2,1)} %broadcast_select_fusion.1), calls=%async_computation | async-start | bytes 16777216 | tf_op jit(solution)/shard_map/all_to_all | solution.py:102
  36.2 0.0 copy-start.3
  36.2 12.7 %copy.39 = bf16[6144,3,256]{0,2,1:T(8,128)(2,1)} copy(bf16[6144,3,256]{2,0,1:T(8,128)(2,1)} %param.12) | data formatting | bytes 18874368 | tf_op args[3]
  48.9 0.0 copy-done.3
  48.9 0.1 dynamic_slice.11
  49.0 0.1 compare_select_fusion.2
  49.1 0.6 gather_fusion
  49.7 0.1 compare_and_fusion
  49.8 0.1 compare_convert_fusion
  49.9 77.8 %all-to-all-done = bf16[8,4,2,256,256]{4,3,2,1,0:T(8,128)(2,1)} async-done(((bf16[8,4,2,256,256]{4,3,2,1,0:T(8,128)(2,1)}), bf16[8,4,2,256,256]{4,3,2,1,0:T(8,128)(2,1)}, u32[]{:S(2)}, u32[]{:S(2)}) %all-to-all-start) | async-done | bytes 8388640 | tf_op jit(solution)/shard_map/all_to_all | solution.py:102
  127.7 8.3 %gather_fusion.2 = bf16[8,4,2,256,256]{4,3,2,1,0:T(8,128)(2,1)} fusion(bf16[8,4,2,256,256]{4,3,2,1,0:T(8,128)(2,1)} %all-to-all-done, s32[1024]{0:T(1024)S(1)} %pad_clamp_fusion), kind=kCustom, calls=%fused_computation.1.clone | custom fusion | bytes 16777248 | tf_op jit(solution)/shard_map/jit(_take)/gather | solution.py:105
  136.0 7.7 %broadcast_select_fusion = bf16[8,4,2,256,256]{4,3,2,1,0:T(8,128)(2,1)} fusion(bf16[8,4,2,256,256]{4,3,2,1,0:T(8,128)(2,1)} %gather_fusion.2, pred[8]{0:T(512)(128)(4,1)S(1)} %get-tuple-element.8), kind=kLoop, calls=%fused_computation.13 | loop fusion | flops 4194304 | bytes 16777224 | tf_op jit(solution)/shard_map/jit(_take)/select_n | solution.py:105
  143.7 7.2 %fusion.43 = (bf16[8,4,1,256,256]{4,3,2,1,0:T(8,128)(2,1)}, f32[8,4,1,256,256]{4,3,2,1,0:T(8,128)}) fusion(bf16[8,4,2,256,256]{4,3,2,1,0:T(8,128)(2,1)} %broadcast_select_fusion), kind=kLoop, calls=%fused_computation.90 | loop fusion | flops 2097152 | bytes 20971520 | tf_op jit(solution)/shard_map/slice | solution.py:51
  151.0 10.8 %reshape.165 = f32[8,1024,2,128]{3,2,1,0:T(2,128)} reshape(f32[8,4,1,256,256]{4,3,2,1,0:T(8,128)} %get-tuple-element.11) | data formatting | bytes 16777216 | tf_op jit(solution)/shard_map/convert_element_type | solution.py:48
  161.7 13.0 %multiply_reduce_fusion = f32[8,1024,2]{2,1,0:T(8,128)} fusion(f32[8,1024,2,128]{3,2,1,0:T(2,128)} %reshape.165), kind=kLoop, calls=%fused_computation.12 | loop fusion | flops 4177920 | bytes 8454144 | tf_op jit(solution)/shard_map/reduce_sum | solution.py:14
  174.7 2.8 %copy.44 = f32[8,1024,2]{1,0,2:T(8,128)S(1)} copy(f32[8,1024,2]{2,1,0:T(8,128)} %multiply_reduce_fusion) | data formatting | bytes 131072 | tf_op jit(solution)/shard_map/reduce_sum | solution.py:14
  177.6 2.6 %copy.45 = f32[8,1024,2]{2,1,0:T(8,128)} copy(f32[8,1024,2]{1,0,2:T(8,128)S(1)} %add_rsqrt_fusion) | data formatting | bytes 131072 | tf_op jit(solution)/shard_map/rsqrt | solution.py:14
  180.2 6.9 %reshape.199 = bf16[8,1024,2,128]{3,2,1,0:T(2,128)(2,1)} reshape(bf16[8,4,1,256,256]{4,3,2,1,0:T(8,128)(2,1)} %get-tuple-element.10) | data formatting | bytes 8388608 | tf_op jit(solution)/shard_map/reshape;squeeze | solution.py:51
  187.1 13.3 %multiply_convert_fusion = bf16[8,1024,2,128]{3,2,1,0:T(2,128)(2,1)} fusion(f32[8,1024,2,128]{3,2,1,0:T(2,128)} %reshape.165, f32[8,1024,2]{2,1,0:T(8,128)} %copy.45), kind=kLoop, calls=%fused_computation.11 | loop fusion | flops 4194304 | bytes 12648448 | tf_op jit(solution)/shard_map/convert_element_type | solution.py:50
  200.4 0.0 all-gather.2.cloned.1.call-done
  200.4 24.1 %fusion = f32[8,256,3,2,128]{1,4,3,2,0:T(8,128)S(1)} fusion(bf16[3,2,128,6144,1]{3,2,1,0,4:T(8,128)(2,1)} %bitcast.40, bf16[8,256,6144]{2,1,0:T(8,128)(2,1)} %all-gather.2.cloned.1.call-done), kind=kOutput, calls=%fused_computation.3 | convolution fusion | flops 19327352832 | bytes 40894464 | tf_op jit(solution)/shard_map/vtd,dk->vtk/dot_general | solution.py:73
  224.6 0.4 multiply_reduce_fusion.2
  225.0 1.0 fusion.13
  226.1 0.0 copy-start
  226.1 0.9 fusion.19
  227.0 1.3 copy-done
  228.3 7.9 %fusion.2 = (f32[8,2,256]{2,1,0:T(2,128)S(1)}, f32[8,2,256,1024]{3,2,1,0:T(8,128)}) fusion(f32[8,1024]{1,0:T(8,128)S(1)} %compare_convert_fusion, bf16[8,1024,2,128]{3,2,1,0:T(2,128)(2,1)S(1)} %copy-done, f32[8,256,3,2,128]{1,4,3,2,0:T(8,128)S(1)} %fusion, f32[8,256,2]{1,2,0:T(2,128)S(1)} %get-tuple-element.17), kind=kOutput, calls=%fused_computation.6 | convolution fusion | flops 1087369216 | bytes 23134208 | tf_op jit(solution)/shard_map/vqhd,vkhd->vhqk/dot_general | solution.py:28
  236.1 10.4 %fusion.21 = bf16[8,256,2,128]{1,3,2,0:T(8,128)(2,1)S(1)} fusion(f32[8,2,128,256]{3,2,1,0:T(8,128)S(1)} %fusion.19, f32[8,2,256,1024]{3,2,1,0:T(8,128)} %get-tuple-element.15, f32[8,1024]{1,0:T(8,128)S(1)} %compare_convert_fusion, bf16[8,1024,2,128]{3,2,1,0:T(2,128)(2,1)} %reshape.199, f32[8,256,2]{1,2,0:T(2,128)S(1)} %add_bitcast_fusion), kind=kOutput, calls=%fused_computation.33 | convolution fusion | flops 1087897600 | bytes 24166400 | tf_op jit(solution)/shard_map/vhqk,vkhd->vqhd/dot_general | solution.py:35
  246.6 1.3 copy.48
  (13 shorter events, 0.1 us)
Async XLA Ops:
  6.5 4.8 %copy-start.1 = (bf16[8,16,6144]{2,1,0:T(8,128)(2,1)S(1)}, bf16[8,16,6144]{2,1,0:T(8,128)(2,1)}, u32[]{:S(2)}) copy-start(bf16[8,16,6144]{2,1,0:T(8,128)(2,1)} %param.9) | copy-start | bytes 4718596
  6.5 193.9 %all-gather.2.cloned.1.call-start = ((), (), s32[]{:S(2)}) async-start(), calls=%async_computation.1 | async-start | bytes 26738688 | tf_op jit(solution)/shard_map/all_gather | solution.py:72
  7.6 6.6 %copy-start.2 = (s32[64]{0:T(128)S(1)}, s32[64]{0:T(128)}, u32[]{:S(2)}) copy-start(s32[64]{0:T(128)} %param.14) | copy-start | bytes 772
  30.9 96.8 %all-to-all-start = ((bf16[8,4,2,256,256]{4,3,2,1,0:T(8,128)(2,1)}), bf16[8,4,2,256,256]{4,3,2,1,0:T(8,128)(2,1)}, u32[]{:S(2)}, u32[]{:S(2)}) async-start(bf16[8,4,2,256,256]{4,3,2,1,0:T(8,128)(2,1)} %broadcast_select_fusion.1), calls=%async_computation | async-start | bytes 16777216 | tf_op jit(solution)/shard_map/all_to_all | solution.py:102
  36.2 12.7 %copy-start.3 = (s32[64]{0:T(128)S(1)}, s32[64]{0:T(128)}, u32[]{:S(2)}) copy-start(s32[64]{0:T(128)} %param.15) | copy-start | bytes 772
  226.1 2.2 copy-start
Sparse Core Ops, SparseCore 0:
  14.3 156.6 all-gather.1
where the time goes:
time: 260 us; the launch traced here: 255 us
  waiting for transfers between devices  77.8 us (30%)
  other arithmetic  58 us (22%)
  local copies, waits for them, and re-layouts  55.8 us (21%)
  matrix products  44.3 us (17%)
  between operations  13.5 us (5%)
  starting transfers between devices  5.24 us (2%)
    all_to_all x1, waiting for transfers between devices, shards(): lax.all_to_all(jnp.take(kv_cache, slot_order, axis=0), 'vid', split_axis=...  77.8 us
    dot_general x1, matrix products, shards(): jnp.einsum('vtd,dk->vtk', rows_piece, weight_matrix, preferred_element_ty...  24.1 us
    unnamed x9, local copies, waits for them, and re-layouts  14 us
    reduce_sum x2, other arithmetic, rms_scale(): jnp.mean(values * values, axis=-1, keepdims=True) + 1e-06  13.4 us
    convert_element_type x1, other arithmetic, split_cache(): previous_keys = rms_scale(blocks[:, :, 0].astype(jnp.float32).reshape(cou...  13.3 us
    dot_general x2, matrix products, attend_group_block(): jnp.einsum('vhqk,vkhd->vqhd', softmax_weights.astype(jnp.bfloat16), group...  11.3 us
    convert_element_type x1, local copies, waits for them, and re-layouts, split_cache(): previous_keys = rms_scale(blocks[:, :, 0].astype(jnp.float32).reshape(cou...  10.8 us
    dot_general x2, matrix products, attend_group_block(): jnp.einsum('vqhd,vkhd->vhqk', query_rows, group_key_rows, preferred_eleme...  8.89 us
  transfers between devices with their start and end apart: 2, of which 1 were waited for; matrix products, arithmetic and copies ran while one was open for 40% of the time, Pallas kernels for 0%

commit v1 on v0

v1 whole, which is shorter than its diff:
```python
import math

import jax
import jax.numpy as jnp
from jax import lax
from jax.experimental import pallas as pl
from jax.experimental.pallas import tpu as pltpu
from jax.sharding import PartitionSpec as P

HEAD = 128
GROUP = 256
MAXC = 4
D = 6144
ROWS = 16
KB = 1024
SCALE = 1.0 / math.sqrt(HEAD)
VMEM = 56 * 1024 * 1024


def rms_scale(values):
    return values * lax.rsqrt(jnp.mean(values * values, axis=-1, keepdims=True) + 1e-06)


def norm_body(first, lat_ref, shift_ref, scale_ref, out_ref):
    v = pl.program_id(0) + first
    x = lat_ref[0].astype(jnp.float32)
    center = jnp.mean(x, axis=-1, keepdims=True)
    offsets = x - center
    spread = jnp.mean(offsets * offsets, axis=-1, keepdims=True)
    gain = 1.0 + scale_ref[pl.ds(v, 1), :]
    out = offsets * lax.rsqrt(spread + 1e-06) * gain + shift_ref[pl.ds(v, 1), :]
    out_ref[0] = out.astype(jnp.bfloat16)


def norm(latents, shift, scale, first, count):
    whole = pl.BlockSpec(shift.shape, lambda i: (0, 0))
    return pl.pallas_call(
        lambda *refs: norm_body(first, *refs),
        grid=(count,),
        in_specs=[
            pl.BlockSpec((1,) + latents.shape[1:], lambda i: (i + first, 0, 0)),
            whole,
            whole,
        ],
        out_specs=pl.BlockSpec((1,) + latents.shape[1:], lambda i: (i, 0, 0)),
        out_shape=jax.ShapeDtypeStruct((count,) + latents.shape[1:], jnp.bfloat16),
        compiler_params=pltpu.CompilerParams(vmem_limit_bytes=VMEM),
        name="norm",
    )(latents, shift, scale)


def reorder(cache, order):
    block = (1,) + cache.shape[1:]
    return pl.pallas_call(
        lambda order_ref, src, dst: dst.__setitem__(..., src[...]),
        grid_spec=pltpu.PrefetchScalarGridSpec(
            num_scalar_prefetch=1,
            grid=(cache.shape[0],),
            in_specs=[pl.BlockSpec(block, lambda i, o: (o[i], 0, 0, 0, 0))],
            out_specs=pl.BlockSpec(block, lambda i, o: (i, 0, 0, 0, 0)),
        ),
        out_shape=jax.ShapeDtypeStruct(cache.shape, cache.dtype),
        compiler_params=pltpu.CompilerParams(vmem_limit_bytes=VMEM),
        name="reorder",
    )(order, cache)


def add_keys(q, keys, values, acc_ref, first):
    logits = lax.dot_general(
        q, keys, (((1,), (1,)), ((), ())), preferred_element_type=jnp.float32
    )
    weights = jnp.exp(logits * SCALE).astype(jnp.bfloat16)
    wide = jnp.concatenate([values, jnp.ones_like(values)], axis=1)
    part = jnp.dot(weights, wide, preferred_element_type=jnp.float32)
    if first:
        acc_ref[...] = part
    else:
        acc_ref[...] += part


def attend_body(chunk, place_ref, count_ref, pos_ref, *refs):
    tokens, (w_ref, kv_a, kv_b, out_ref, acc_ref, sum_ref) = refs[:8], refs[8:]
    k = pl.program_id(0)

    @pl.when(k == 0)
    def _():
        acc_ref[...] = jnp.zeros_like(acc_ref)

    x = jnp.concatenate([t[...] for t in tokens], axis=0)
    for j in range(3):
        acc_ref[j] += jnp.dot(x, w_ref[j], preferred_element_type=jnp.float32)

    @pl.when(k == pl.num_programs(0) - 1)
    def _():
        y, z, sign = pos_ref[0], pos_ref[1], pos_ref[2]
        for i, kv in ((0, kv_a), (1, kv_b)):
            rows = pl.ds(i * GROUP, GROUP)
            live = count_ref[chunk + 4 * i]
            queries = []
            for h in range(2):
                lanes = pl.ds(h * HEAD, HEAD)
                q = rms_scale(acc_ref[0, rows, lanes]).astype(jnp.bfloat16)
                key = rms_scale(acc_ref[1, rows, lanes]).astype(jnp.bfloat16)
                add_keys(q, key, acc_ref[2, rows, lanes].astype(jnp.bfloat16), sum_ref.at[h], True)
                queries.append(q)
            for g in range(MAXC):

                @pl.when(g < live)
                def _():
                    for h in range(2):
                        lanes = pl.ds(h * HEAD, HEAD)
                        old = rms_scale(kv[0, g, 0, :, lanes].astype(jnp.float32))
                        add_keys(
                            queries[h],
                            old.astype(jnp.bfloat16),
                            kv[0, g, 1, :, lanes],
                            sum_ref.at[h],
                            False,
                        )

            out = jnp.concatenate(
                [sum_ref[h, :, :HEAD] / sum_ref[h, :, HEAD:] for h in range(2)], axis=1
            ).astype(jnp.bfloat16)
            for outer in range(4):
                for inner in range(4):
                    a = (y - sign * (inner if i == 0 else outer)) & 3
                    b = (z - sign * (outer if i == 0 else inner)) & 3
                    start = pl.multiple_of((a * 4 + b) * ROWS, ROWS)
                    at = (outer * 4 + inner) * ROWS
                    out_ref[i, pl.ds(start, ROWS), :] = out[at : at + ROWS]


def attend(chunk, tokens, weights, cache, places, counts, pos):
    kv_block = (1,) + cache.shape[1:]
    token_spec = pl.BlockSpec((4 * ROWS, KB), lambda k, *s: (0, k))
    return pl.pallas_call(
        lambda *refs: attend_body(chunk, *refs),
        grid_spec=pltpu.PrefetchScalarGridSpec(
            num_scalar_prefetch=3,
            grid=(D // KB,),
            in_specs=[token_spec] * 8
            + [
                pl.BlockSpec((3, KB, 2 * HEAD), lambda k, *s: (0, k, 0)),
                pl.BlockSpec(kv_block, lambda k, p, c, q: (p[chunk], 0, 0, 0, 0)),
                pl.BlockSpec(kv_block, lambda k, p, c, q: (p[chunk + 4], 0, 0, 0, 0)),
            ],
            out_specs=pl.BlockSpec((2, GROUP, 2 * HEAD), lambda k, *s: (0, 0, 0)),
            scratch_shapes=[
                pltpu.VMEM((3, 2 * GROUP, 2 * HEAD), jnp.float32),
                pltpu.VMEM((2, GROUP, 2 * HEAD), jnp.float32),
            ],
        ),
        out_shape=jax.ShapeDtypeStruct((2, GROUP, 2 * HEAD), jnp.bfloat16),
        compiler_params=pltpu.CompilerParams(vmem_limit_bytes=VMEM),
        cost_estimate=pl.CostEstimate(
            flops=2 * 512 * D * 768, bytes_accessed=18 << 20, transcendentals=1 << 20
        ),
        name="attend",
    )(places, counts, pos, *tokens, weights, cache, cache)


def ring(dy, dz):
    pairs = []
    for vid in range(8):
        s = 1 if vid % 2 == 0 else -1
        for y in range(4):
            for z in range(4):
                to = (y + s * dy) % 4 * 4 + (z + s * dz) % 4
                pairs.append((vid * 16 + y * 4 + z, vid * 16 + to))
    return pairs


def send(value, pairs):
    return lax.ppermute(value, ("vid", "fsdp"), pairs)


def shards(latents, shift_mod, scale_mod, qkv_weight, kv_cache, holders, cached):
    vid = lax.axis_index("vid")
    fsdp = lax.axis_index("fsdp")
    along_y, along_z = ring(1, 0), ring(0, 1)
    weights = jnp.transpose(qkv_weight, (1, 0, 2))

    ya = [norm(latents, shift_mod, scale_mod, 0, 4)]
    zb = [norm(latents, shift_mod, scale_mod, 4, 4)]
    for _ in range(3):
        ya.append(send(ya[-1], along_y))
        zb.append(send(zb[-1], along_z))

    by_owner = holders.reshape(8, 8)
    order = jnp.sum(jnp.where(by_owner // 8 == vid, by_owner % 8, 0), axis=1, dtype=jnp.int32)
    places = lax.dynamic_slice_in_dim(holders, vid * 8, 8) // 8
    counts = lax.dynamic_slice_in_dim(cached, vid * 8, 8)
    pos = jnp.stack([fsdp // 4, fsdp % 4, 1 - 2 * (vid % 2)]).astype(jnp.int32)
    cache = lax.all_to_all(
        reorder(kv_cache, order), "vid", split_axis=0, concat_axis=0, tiled=True
    )

    outs = []
    for c in range(4):
        a = [jnp.concatenate([block[c] for block in ya], axis=0)]
        b = [jnp.concatenate([block[c] for block in zb], axis=0)]
        for _ in range(3):
            a.append(send(a[-1], along_z))
            b.append(send(b[-1], along_y))
        outs.append(attend(c, a + b, weights, cache, places, counts, pos))
    return jnp.concatenate([o[:1] for o in outs] + [o[1:] for o in outs], axis=0)


def solution(mesh):
    return jax.shard_map(
        shards,
        mesh=mesh,
        in_specs=(
            P("vid", "fsdp", None),
            P("vid", None),
            P("vid", None),
            P(None, None, "fsdp"),
            P("vid", None, None, None, "fsdp"),
            P(),
            P(),
        ),
        out_specs=P("vid", None, "fsdp"),
        check_vma=False,
    )
```

time: 260 us -> 210 us (0.81); the launches traced: 255 us -> 209 us
  Pallas kernels: 0 us -> 80 us
  other arithmetic: 58 us -> 2.34 us
  matrix products: 44.3 us -> 0 us
  local copies, waits for them, and re-layouts: 55.8 us -> 14.6 us
  starting transfers between devices: 5.24 us -> 20.4 us
  waiting for transfers between devices: 77.8 us -> 91.4 us
  between operations: 13.5 us -> 0.46 us
    ppermute x0 -> x30, waiting for transfers between devices: none -> 91.4 us  [send(): return lax.ppermute(value, ('vid', 'fsdp'), pairs)]
    pallas_call x0 -> x7, Pallas kernels: none -> 80 us  [the longest x4 62.1 us: attend(): pl.pallas_call(lambda *refs: attend_body(chunk, *refs), grid_spec=pltpu.P...]
    all_to_all x1, waiting for transfers between devices: 77.8 us -> 0.01 us  [shards(): lax.all_to_all(reorder(kv_cache, order), 'vid', split_axis=0, concat_axis...]
    dot_general x5 -> x0, matrix products: 44.3 us -> none  [the longest x1 24.1 us: shards(): jnp.einsum('vtd,dk->vtk', rows_piece, weight_matrix, preferred_element_ty...]
    gather x3 -> x0, local copies, waits for them, and re-layouts: 17.1 us -> none  [the longest x1 8.33 us: shards(): received_blocks = jnp.take(arrived, video_places, axis=0)]
    reduce_sum x7 -> x1, other arithmetic: 17.5 us -> 0.7 us  [shards(): jnp.sum(jnp.where(by_owner // 8 == vid, by_owner % 8, 0), axis=1, dtype=j...]
    convert_element_type x3 -> x0, other arithmetic: 16.2 us -> none  [the longest x1 13.3 us: split_cache(): previous_keys = rms_scale(blocks[:, :, 0].astype(jnp.float32).reshape(cou...]
    select_n x6 -> x1, other arithmetic: 15.8 us -> 0.56 us  [shards(): places = lax.dynamic_slice_in_dim(holders, vid * 8, 8) // 8]
  transfers between devices with their start and end apart: 2 -> 31, of which waited for: 1 -> 16; matrix products, arithmetic and copies ran while one was open for 40% -> 3% of each run, Pallas kernels for 0% -> 29%
where the time goes in v1:
time: 210 us; the launch traced here: 209 us
  waiting for transfers between devices  91.4 us (44%)
  Pallas kernels  80 us (38%)
  starting transfers between devices  20.4 us (10%)
  local copies, waits for them, and re-layouts  14.6 us (7%)
  other arithmetic  2.34 us (1%)
    ppermute x30, waiting for transfers between devices, send(): return lax.ppermute(value, ('vid', 'fsdp'), pairs)  91.4 us
    pallas_call x4, Pallas kernels, attend(): pl.pallas_call(lambda *refs: attend_body(chunk, *refs), grid_spec=pltpu.P...  62.1 us
    ppermute x30, starting transfers between devices, send(): return lax.ppermute(value, ('vid', 'fsdp'), pairs)  13 us
    unnamed x65, local copies, waits for them, and re-layouts  11.8 us
    pallas_call x1, Pallas kernels, reorder(): pl.pallas_call(lambda order_ref, src, dst: dst.__setitem__(..., src[...])...  9.63 us
    pallas_call x2, Pallas kernels, norm(): pl.pallas_call(lambda *refs: norm_body(first, *refs), grid=(count,), in_s...  8.24 us
    all_to_all x1, starting transfers between devices, shards(): lax.all_to_all(reorder(kv_cache, order), 'vid', split_axis=0, concat_axis...  7.37 us
  transfers between devices with their start and end apart: 31, of which 16 were waited for; matrix products, arithmetic and copies ran while one was open for 3% of the time, Pallas kernels for 29%

profile of v1, /device:TPU:4, one launch (start us, length us, event | category | flops | bytes accessed | tf_op | source)
XLA Modules:
  0.0 209.1 jit_solution(10647889689165777517)
XLA Ops:
  0.0 4.1 %norm.2 = bf16[4,16,6144]{2,1,0:T(8,128)(2,1)} custom-call(bf16[8,16,6144]{2,1,0:T(8,128)(2,1)} %refs_0_.3, f32[8,6144]{1,0:T(8,128)} %refs_1_.3, f32[8,6144]{1,0:T(8,128)} %refs_2_.3), custom_call_target="tpu_custom_call" | custom-call | tf_op jit(solution)/shard_map/norm/pallas_call | solution.py:37
  4.1 1.6 collective-permute-start
  5.7 4.1 %norm.3 = bf16[4,16,6144]{2,1,0:T(8,128)(2,1)} custom-call(bf16[8,16,6144]{2,1,0:T(8,128)(2,1)} %refs_0_.3, f32[8,6144]{1,0:T(8,128)} %refs_1_.3, f32[8,6144]{1,0:T(8,128)} %refs_2_.3), custom_call_target="tpu_custom_call" | custom-call | tf_op jit(solution)/shard_map/norm/pallas_call | solution.py:37
  9.8 1.9 collective-permute-start.6
  11.7 0.1 reshape.3
  11.8 0.7 fusion.2.order_ref
  12.5 9.6 %reorder.1 = bf16[8,4,2,256,256]{4,3,2,1,0:T(8,128)(2,1)} custom-call(s32[8]{0:T(128)} %fusion.2.order_ref, bf16[8,4,2,256,256]{4,3,2,1,0:T(8,128)(2,1)} %src.1), custom_call_target="tpu_custom_call" | custom-call | tf_op jit(solution)/shard_map/reorder/pallas_call | solution.py:54
  22.2 7.4 %all-to-all-start = ((bf16[8,4,2,256,256]{4,3,2,1,0:T(8,128)(2,1)}), bf16[8,4,2,256,256]{4,3,2,1,0:T(8,128)(2,1)}, u32[]{:S(2)}, u32[]{:S(2)}) async-start(bf16[8,4,2,256,256]{4,3,2,1,0:T(8,128)(2,1)} %reorder.1), calls=%async_computation | async-start | bytes 16777216 | tf_op jit(solution)/shard_map/all_to_all | solution.py:194
  29.6 1.1 copy-done
  30.7 0.1 collective-permute-start.1
  30.8 0.1 slice_bitcast_fusion.6
  30.9 1.7 collective-permute-start.7
  32.6 11.4 %collective-permute-done.1 = bf16[4,16,6144]{2,1,0:T(8,128)(2,1)S(1)} collective-permute-done((bf16[4,16,6144]{2,1,0:T(8,128)(2,1)S(1)}, bf16[4,16,6144]{2,1,0:T(8,128)(2,1)S(1)}, u32[]{:S(2)}, u32[]{:S(2)}) %collective-permute-start.1) | collective-permute-done | bytes 786464 | tf_op jit(solution)/shard_map/ppermute | solution.py:174
  44.1 0.1 collective-permute-done.7
  44.2 0.4 collective-permute-start.8
  44.6 12.6 %collective-permute-done.2 = bf16[4,16,6144]{2,1,0:T(8,128)(2,1)S(1)} collective-permute-done((bf16[4,16,6144]{2,1,0:T(8,128)(2,1)S(1)}, bf16[4,16,6144]{2,1,0:T(8,128)(2,1)S(1)}, u32[]{:S(2)}, u32[]{:S(2)}) %collective-permute-start.2) | collective-permute-done | bytes 786464 | tf_op jit(solution)/shard_map/ppermute | solution.py:174
  57.3 0.1 pad_maximum_fusion.6.refs_3_
  57.3 0.1 collective-permute-start.24
  57.6 0.6 copy-done.2
  58.2 0.3 collective-permute-start.27
  58.6 0.8 collective-permute-start.18
  59.5 0.5 collective-permute-start.9
  60.1 0.7 collective-permute-start.3
  60.9 0.1 pad_maximum_fusion.2.refs_3_
  61.0 9.6 %collective-permute-done.24.refs_4_ = bf16[64,6144]{1,0:T(8,128)(2,1)S(1)} collective-permute-done((bf16[64,6144]{1,0:T(8,128)(2,1)S(1)}, bf16[64,6144]{1,0:T(8,128)(2,1)S(1)}, u32[]{:S(2)}, u32[]{:S(2)}) %collective-permute-start.24) | collective-permute-done | bytes 786464 | tf_op jit(solution)/shard_map/ppermute | solution.py:174
  70.6 0.8 collective-permute-done.27.refs_8_
  71.4 1.1 collective-permute-start.12
  72.6 6.4 %collective-permute-done.18.refs_4_ = bf16[64,6144]{1,0:T(8,128)(2,1)S(1)} collective-permute-done((bf16[64,6144]{1,0:T(8,128)(2,1)S(1)}, bf16[64,6144]{1,0:T(8,128)(2,1)S(1)}, u32[]{:S(2)}, u32[]{:S(2)}) %collective-permute-start.18) | collective-permute-done | bytes 786464 | tf_op jit(solution)/shard_map/ppermute | solution.py:174
  79.0 0.8 collective-permute-done.9.refs_8_
  79.9 7.6 %collective-permute-done.3.refs_4_ = bf16[64,6144]{1,0:T(8,128)(2,1)S(1)} collective-permute-done((bf16[64,6144]{1,0:T(8,128)(2,1)S(1)}, bf16[64,6144]{1,0:T(8,128)(2,1)S(1)}, u32[]{:S(2)}, u32[]{:S(2)}) %collective-permute-start.3) | collective-permute-done | bytes 786464 | tf_op jit(solution)/shard_map/ppermute | solution.py:174
  87.5 0.9 collective-permute-done.21.refs_8_
  88.4 1.1 collective-permute-start.25
  89.5 6.4 %collective-permute-done.12.refs_4_ = bf16[64,6144]{1,0:T(8,128)(2,1)S(1)} collective-permute-done((bf16[64,6144]{1,0:T(8,128)(2,1)S(1)}, bf16[64,6144]{1,0:T(8,128)(2,1)S(1)}, u32[]{:S(2)}, u32[]{:S(2)}) %collective-permute-start.12) | collective-permute-done | bytes 786464 | tf_op jit(solution)/shard_map/ppermute | solution.py:174
  95.9 0.9 collective-permute-done.15.refs_8_
  96.8 8.4 %collective-permute-done.10.refs_9_ = bf16[64,6144]{1,0:T(8,128)(2,1)} collective-permute-done((bf16[64,6144]{1,0:T(8,128)(2,1)S(1)}, bf16[64,6144]{1,0:T(8,128)(2,1)}, u32[]{:S(2)}, u32[]{:S(2)}) %collective-permute-start.10) | collective-permute-done | bytes 786464 | tf_op jit(solution)/shard_map/ppermute | solution.py:174
  105.3 1.1 collective-permute-start.5
  106.3 6.4 %collective-permute-done.25.refs_5_ = bf16[64,6144]{1,0:T(8,128)(2,1)S(1)} collective-permute-done((bf16[64,6144]{1,0:T(8,128)(2,1)S(1)}, bf16[64,6144]{1,0:T(8,128)(2,1)S(1)}, u32[]{:S(2)}, u32[]{:S(2)}) %collective-permute-start.25) | collective-permute-done | bytes 786464 | tf_op jit(solution)/shard_map/ppermute | solution.py:174
  112.7 0.9 copy-done.16
  113.7 7.5 %collective-permute-done.13.refs_5_ = bf16[64,6144]{1,0:T(8,128)(2,1)S(1)} collective-permute-done((bf16[64,6144]{1,0:T(8,128)(2,1)S(1)}, bf16[64,6144]{1,0:T(8,128)(2,1)S(1)}, u32[]{:S(2)}, u32[]{:S(2)}) %collective-permute-start.13) | collective-permute-done | bytes 786464 | tf_op jit(solution)/shard_map/ppermute | solution.py:174
  121.2 0.9 copy-done.21
  122.1 0.7 dynamic_slice.7.refs_1_
  122.7 0.6 and_select_fusion.refs_0_
  123.3 0.1 collective-permute-start.14
  123.4 6.3 %collective-permute-done.5.refs_6_ = bf16[64,6144]{1,0:T(8,128)(2,1)} collective-permute-done((bf16[64,6144]{1,0:T(8,128)(2,1)}, bf16[64,6144]{1,0:T(8,128)(2,1)}, u32[]{:S(2)}, u32[]{:S(2)}) %collective-permute-start.5) | collective-permute-done | bytes 786464 | tf_op jit(solution)/shard_map/ppermute | solution.py:174
  129.7 0.7 pad_add_fusion.refs_2_
  130.4 14.4 %attend.4 = bf16[2,256,256]{2,1,0:T(8,128)(2,1)} custom-call(s32[8]{0:T(128)} %and_select_fusion.refs_0_, s32[8]{0:T(128)} %dynamic_slice.7.refs_1_, s32[3]{0:T(128)} %pad_add_fusion.refs_2_, bf16[64,6144]{1,0:T(8,128)(2,1)} %copy-done.8, bf16[64,6144]{1,0:T(8,128)(2,1)} %copy-done.20, bf16[64,6144]{1,0:T(8,128)(2,1)} %collective-permute-done.4.refs_5_, ...), custom_call_target="tpu_custom_call" | custom-call | flops 4831838208 | bytes 18874368 | tf_op jit(solution)/shard_map/attend/pallas_call | solution.py:136
  144.8 0.1 collective-permute-start.20
  144.9 0.1 collective-permute-start.23
  145.0 0.9 slice_dynamic-update-slice_fusion.7
  145.9 0.9 collective-permute-start.26
  146.8 0.5 collective-permute-start.29
  147.3 5.1 %collective-permute-done.17.refs_10_ = bf16[64,6144]{1,0:T(8,128)(2,1)} collective-permute-done((bf16[64,6144]{1,0:T(8,128)(2,1)}, bf16[64,6144]{1,0:T(8,128)(2,1)}, u32[]{:S(2)}, u32[]{:S(2)}) %collective-permute-start.17) | collective-permute-done | bytes 786464 | tf_op jit(solution)/shard_map/ppermute | solution.py:174
  152.4 16.8 %attend.5 = bf16[2,256,256]{2,1,0:T(8,128)(2,1)} custom-call(s32[8]{0:T(128)} %and_select_fusion.refs_0_, s32[8]{0:T(128)} %dynamic_slice.7.refs_1_, s32[3]{0:T(128)} %pad_add_fusion.refs_2_, bf16[64,6144]{1,0:T(8,128)(2,1)} %copy-done.6, bf16[64,6144]{1,0:T(8,128)(2,1)} %copy-done.18, bf16[64,6144]{1,0:T(8,128)(2,1)} %copy-done.21, ...), custom_call_target="tpu_custom_call" | custom-call | flops 4831838208 | bytes 18874368 | tf_op jit(solution)/shard_map/attend/pallas_call | solution.py:136
  169.2 0.9 slice_dynamic-update-slice_fusion.6
  170.2 0.9 copy-done.23
  171.0 0.9 copy-done.25
  172.0 15.3 %attend.6 = bf16[2,256,256]{2,1,0:T(8,128)(2,1)} custom-call(s32[8]{0:T(128)} %and_select_fusion.refs_0_, s32[8]{0:T(128)} %dynamic_slice.7.refs_1_, s32[3]{0:T(128)} %pad_add_fusion.refs_2_, bf16[64,6144]{1,0:T(8,128)(2,1)} %copy-done.4, bf16[64,6144]{1,0:T(8,128)(2,1)} %copy-done.15, bf16[64,6144]{1,0:T(8,128)(2,1)} %collective-permute-done.19.refs_5_, ...), custom_call_target="tpu_custom_call" | custom-call | flops 4831838208 | bytes 18874368 | tf_op jit(solution)/shard_map/attend/pallas_call | solution.py:136
  187.3 0.9 slice_dynamic-update-slice_fusion.5
  188.3 0.9 copy-done.22
  189.1 0.9 copy-done.24
  190.0 15.6 %attend.7 = bf16[2,256,256]{2,1,0:T(8,128)(2,1)} custom-call(s32[8]{0:T(128)} %and_select_fusion.refs_0_, s32[8]{0:T(128)} %dynamic_slice.7.refs_1_, s32[3]{0:T(128)} %pad_add_fusion.refs_2_, bf16[64,6144]{1,0:T(8,128)(2,1)} %copy-done.2, bf16[64,6144]{1,0:T(8,128)(2,1)} %copy-done.13, bf16[64,6144]{1,0:T(8,128)(2,1)} %copy-done.16, ...), custom_call_target="tpu_custom_call" | custom-call | flops 4831838208 | bytes 18874368 | tf_op jit(solution)/shard_map/attend/pallas_call | solution.py:136
  205.6 0.9 slice_dynamic-update-slice_fusion.4
  206.6 1.0 copy-done.26
  207.6 1.6 slice_dynamic-update-slice_fusion
  (92 shorter events, 0.9 us)
Async XLA Ops:
  4.1 7.6 %copy-start.27 = (s32[64]{0:T(128)S(1)}, s32[64]{0:T(128)}, u32[]{:S(2)}) copy-start(s32[64]{0:T(128)} %param.12) | copy-start | bytes 772
  4.1 26.6 %collective-permute-start = (bf16[4,16,6144]{2,1,0:T(8,128)(2,1)}, bf16[4,16,6144]{2,1,0:T(8,128)(2,1)S(1)}, u32[]{:S(2)}, u32[]{:S(2)}) collective-permute-start(bf16[4,16,6144]{2,1,0:T(8,128)(2,1)} %norm.2), channel_id=1, source_target_pairs={{0,4},{1,5},{2,6},{3,7},{4,8},{5,9},{6,10},{7,11},{8,12},{9,13},{1... | collective-permute-start | bytes 2359304 | tf_op jit(solution)/shard_map/ppermute | solution.py:174
  9.8 21.1 %collective-permute-start.6 = (bf16[4,16,6144]{2,1,0:T(8,128)(2,1)}, bf16[4,16,6144]{2,1,0:T(8,128)(2,1)S(1)}, u32[]{:S(2)}, u32[]{:S(2)}) collective-permute-start(bf16[4,16,6144]{2,1,0:T(8,128)(2,1)} %norm.3), channel_id=1, source_target_pairs={{0,1},{1,2},{2,3},{3,0},{4,5},{5,6},{6,7},{7,4},{8,9},{9,10},{10,1... | collective-permute-start | bytes 2359304 | tf_op jit(solution)/shard_map/ppermute | solution.py:174
  22.2 7.4 %copy-start.1 = (bf16[4,16,6144]{2,1,0:T(8,128)(2,1)S(1)}, bf16[4,16,6144]{2,1,0:T(8,128)(2,1)}, u32[]{:S(2)}) copy-start(bf16[4,16,6144]{2,1,0:T(8,128)(2,1)} %norm.2) | copy-start | bytes 2359300
  22.2 108.2 %all-to-all-start = ((bf16[8,4,2,256,256]{4,3,2,1,0:T(8,128)(2,1)}), bf16[8,4,2,256,256]{4,3,2,1,0:T(8,128)(2,1)}, u32[]{:S(2)}, u32[]{:S(2)}) async-start(bf16[8,4,2,256,256]{4,3,2,1,0:T(8,128)(2,1)} %reorder.1), calls=%async_computation | async-start | bytes 16777216 | tf_op jit(solution)/shard_map/all_to_all | solution.py:194
  29.5 1.1 copy-start
  30.7 13.3 %collective-permute-start.1 = (bf16[4,16,6144]{2,1,0:T(8,128)(2,1)S(1)}, bf16[4,16,6144]{2,1,0:T(8,128)(2,1)S(1)}, u32[]{:S(2)}, u32[]{:S(2)}) collective-permute-start(bf16[4,16,6144]{2,1,0:T(8,128)(2,1)S(1)} %collective-permute-done), channel_id=1, source_target_pairs={{0,4},{1,5},{2,6},{3,7},{4,8},{5,9},{6,10},{7,11},{8,12},{9,13},{1... | collective-permute-start | bytes 2359304 | tf_op jit(solution)/shard_map/ppermute | solution.py:174
  30.9 13.3 %collective-permute-start.7 = (bf16[4,16,6144]{2,1,0:T(8,128)(2,1)S(1)}, bf16[4,16,6144]{2,1,0:T(8,128)(2,1)S(1)}, u32[]{:S(2)}, u32[]{:S(2)}) collective-permute-start(bf16[4,16,6144]{2,1,0:T(8,128)(2,1)S(1)} %collective-permute-done.6), channel_id=1, source_target_pairs={{0,1},{1,2},{2,3},{3,0},{4,5},{5,6},{6,7},{7,4},{8,9},{9,10},{10,1... | collective-permute-start | bytes 2359304 | tf_op jit(solution)/shard_map/ppermute | solution.py:174
  44.0 13.2 %collective-permute-start.2 = (bf16[4,16,6144]{2,1,0:T(8,128)(2,1)S(1)}, bf16[4,16,6144]{2,1,0:T(8,128)(2,1)S(1)}, u32[]{:S(2)}, u32[]{:S(2)}) collective-permute-start(bf16[4,16,6144]{2,1,0:T(8,128)(2,1)S(1)} %collective-permute-done.1), channel_id=1, source_target_pairs={{0,4},{1,5},{2,6},{3,7},{4,8},{5,9},{6,10},{7,11},{8,12},{9,13},{1... | collective-permute-start | bytes 2359304 | tf_op jit(solution)/shard_map/ppermute | solution.py:174
  44.2 13.3 %collective-permute-start.8 = (bf16[4,16,6144]{2,1,0:T(8,128)(2,1)S(1)}, bf16[4,16,6144]{2,1,0:T(8,128)(2,1)S(1)}, u32[]{:S(2)}, u32[]{:S(2)}) collective-permute-start(bf16[4,16,6144]{2,1,0:T(8,128)(2,1)S(1)} %collective-permute-done.7), channel_id=1, source_target_pairs={{0,1},{1,2},{2,3},{3,0},{4,5},{5,6},{6,7},{7,4},{8,9},{9,10},{10,1... | collective-permute-start | bytes 2359304 | tf_op jit(solution)/shard_map/ppermute | solution.py:174
  57.3 0.9 copy-start.2
  57.3 13.3 %collective-permute-start.24 = (bf16[64,6144]{1,0:T(8,128)(2,1)S(1)}, bf16[64,6144]{1,0:T(8,128)(2,1)S(1)}, u32[]{:S(2)}, u32[]{:S(2)}) collective-permute-start(bf16[64,6144]{1,0:T(8,128)(2,1)S(1)} %pad_maximum_fusion.6.refs_3_), channel_id=1, source_target_pairs={{0,1},{1,2},{2,3},{3,0},{4,5},{5,6},{6,7},{7,4},{8,9},{9,10},{10,1... | collective-permute-start | bytes 2359304 | tf_op jit(solution)/shard_map/ppermute | solution.py:174
  58.2 1.3 copy-start.3
  58.2 13.2 %collective-permute-start.27 = (bf16[64,6144]{1,0:T(8,128)(2,1)S(1)}, bf16[64,6144]{1,0:T(8,128)(2,1)S(1)}, u32[]{:S(2)}, u32[]{:S(2)}) collective-permute-start(bf16[64,6144]{1,0:T(8,128)(2,1)S(1)} %pad_maximum_fusion.7.refs_7_), channel_id=1, source_target_pairs={{0,4},{1,5},{2,6},{3,7},{4,8},{5,9},{6,10},{7,11},{8,12},{9,13},{1... | collective-permute-start | bytes 2359304 | tf_op jit(solution)/shard_map/ppermute | solution.py:174
  58.6 1.5 copy-start.4
  58.6 20.4 %collective-permute-start.18 = (bf16[64,6144]{1,0:T(8,128)(2,1)S(1)}, bf16[64,6144]{1,0:T(8,128)(2,1)S(1)}, u32[]{:S(2)}, u32[]{:S(2)}) collective-permute-start(bf16[64,6144]{1,0:T(8,128)(2,1)S(1)} %pad_maximum_fusion.4.refs_3_), channel_id=1, source_target_pairs={{0,1},{1,2},{2,3},{3,0},{4,5},{5,6},{6,7},{7,4},{8,9},{9,10},{10,1... | collective-permute-start | bytes 2359304 | tf_op jit(solution)/shard_map/ppermute | solution.py:174
  59.5 1.3 copy-start.7
  59.5 20.3 %collective-permute-start.9 = (bf16[64,6144]{1,0:T(8,128)(2,1)S(1)}, bf16[64,6144]{1,0:T(8,128)(2,1)S(1)}, u32[]{:S(2)}, u32[]{:S(2)}) collective-permute-start(bf16[64,6144]{1,0:T(8,128)(2,1)S(1)} %pad_maximum_fusion.1.refs_7_), channel_id=1, source_target_pairs={{0,4},{1,5},{2,6},{3,7},{4,8},{5,9},{6,10},{7,11},{8,12},{9,13},{1... | collective-permute-start | bytes 2359304 | tf_op jit(solution)/shard_map/ppermute | solution.py:174
  60.1 0.9 copy-start.8
  60.1 27.4 %collective-permute-start.3 = (bf16[64,6144]{1,0:T(8,128)(2,1)S(1)}, bf16[64,6144]{1,0:T(8,128)(2,1)S(1)}, u32[]{:S(2)}, u32[]{:S(2)}) collective-permute-start(bf16[64,6144]{1,0:T(8,128)(2,1)S(1)} %pad_maximum_fusion.refs_3_), channel_id=1, source_target_pairs={{0,1},{1,2},{2,3},{3,0},{4,5},{5,6},{6,7},{7,4},{8,9},{9,10},{10,1... | collective-permute-start | bytes 2359304 | tf_op jit(solution)/shard_map/ppermute | solution.py:174
  60.9 11.7 %copy-start.5 = (bf16[64,6144]{1,0:T(8,128)(2,1)}, bf16[64,6144]{1,0:T(8,128)(2,1)S(1)}, u32[]{:S(2)}) copy-start(bf16[64,6144]{1,0:T(8,128)(2,1)S(1)} %pad_maximum_fusion.5.refs_7_) | copy-start | bytes 2359300
  60.9 61.2 %copy-start.28 = (s32[64]{0:T(128)S(1)}, s32[64]{0:T(128)}, u32[]{:S(2)}) copy-start(s32[64]{0:T(128)} %param.13) | copy-start | bytes 772
  61.0 27.4 %copy-start.6 = (bf16[64,6144]{1,0:T(8,128)(2,1)}, bf16[64,6144]{1,0:T(8,128)(2,1)S(1)}, u32[]{:S(2)}) copy-start(bf16[64,6144]{1,0:T(8,128)(2,1)S(1)} %pad_maximum_fusion.2.refs_3_) | copy-start | bytes 2359300
  70.6 74.2 %copy-start.13 = (bf16[64,6144]{1,0:T(8,128)(2,1)}, bf16[64,6144]{1,0:T(8,128)(2,1)S(1)}, u32[]{:S(2)}) copy-start(bf16[64,6144]{1,0:T(8,128)(2,1)S(1)} %collective-permute-done.24.refs_4_) | copy-start | bytes 2359300
  70.6 17.8 %collective-permute-start.21 = (bf16[64,6144]{1,0:T(8,128)(2,1)S(1)}, bf16[64,6144]{1,0:T(8,128)(2,1)}, u32[]{:S(2)}, u32[]{:S(2)}) collective-permute-start(bf16[64,6144]{1,0:T(8,128)(2,1)S(1)} %pad_maximum_fusion.5.refs_7_), channel_id=1, source_target_pairs={{0,4},{1,5},{2,6},{3,7},{4,8},{5,9},{6,10},{7,11},{8,12},{9,13},{1... | collective-permute-start | bytes 2359304 | tf_op jit(solution)/shard_map/ppermute | solution.py:174
  71.4 73.3 %copy-start.14 = (bf16[64,6144]{1,0:T(8,128)(2,1)}, bf16[64,6144]{1,0:T(8,128)(2,1)S(1)}, u32[]{:S(2)}) copy-start(bf16[64,6144]{1,0:T(8,128)(2,1)S(1)} %collective-permute-done.27.refs_8_) | copy-start | bytes 2359300
  71.4 24.4 %collective-permute-start.12 = (bf16[64,6144]{1,0:T(8,128)(2,1)S(1)}, bf16[64,6144]{1,0:T(8,128)(2,1)S(1)}, u32[]{:S(2)}, u32[]{:S(2)}) collective-permute-start(bf16[64,6144]{1,0:T(8,128)(2,1)S(1)} %pad_maximum_fusion.2.refs_3_), channel_id=1, source_target_pairs={{0,1},{1,2},{2,3},{3,0},{4,5},{5,6},{6,7},{7,4},{8,9},{9,10},{10,1... | collective-permute-start | bytes 2359304 | tf_op jit(solution)/shard_map/ppermute | solution.py:174
  72.6 72.2 %copy-start.9 = (bf16[64,6144]{1,0:T(8,128)(2,1)}, bf16[64,6144]{1,0:T(8,128)(2,1)S(1)}, u32[]{:S(2)}) copy-start(bf16[64,6144]{1,0:T(8,128)(2,1)S(1)} %pad_maximum_fusion.3.refs_7_) | copy-start | bytes 2359300
  79.0 65.8 %copy-start.15 = (bf16[64,6144]{1,0:T(8,128)(2,1)}, bf16[64,6144]{1,0:T(8,128)(2,1)S(1)}, u32[]{:S(2)}) copy-start(bf16[64,6144]{1,0:T(8,128)(2,1)S(1)} %collective-permute-done.18.refs_4_) | copy-start | bytes 2359300
  79.0 17.8 %collective-permute-start.15 = (bf16[64,6144]{1,0:T(8,128)(2,1)S(1)}, bf16[64,6144]{1,0:T(8,128)(2,1)}, u32[]{:S(2)}, u32[]{:S(2)}) collective-permute-start(bf16[64,6144]{1,0:T(8,128)(2,1)S(1)} %pad_maximum_fusion.3.refs_7_), channel_id=1, source_target_pairs={{0,4},{1,5},{2,6},{3,7},{4,8},{5,9},{6,10},{7,11},{8,12},{9,13},{1... | collective-permute-start | bytes 2359304 | tf_op jit(solution)/shard_map/ppermute | solution.py:174
  79.9 41.3 %copy-start.19 = (bf16[64,6144]{1,0:T(8,128)(2,1)}, bf16[64,6144]{1,0:T(8,128)(2,1)S(1)}, u32[]{:S(2)}) copy-start(bf16[64,6144]{1,0:T(8,128)(2,1)S(1)} %collective-permute-done.9.refs_8_) | copy-start | bytes 2359300
  79.9 25.4 %collective-permute-start.10 = (bf16[64,6144]{1,0:T(8,128)(2,1)S(1)}, bf16[64,6144]{1,0:T(8,128)(2,1)}, u32[]{:S(2)}, u32[]{:S(2)}) collective-permute-start(bf16[64,6144]{1,0:T(8,128)(2,1)S(1)} %collective-permute-done.9.refs_8_), channel_id=1, source_target_pairs={{0,4},{1,5},{2,6},{3,7},{4,8},{5,9},{6,10},{7,11},{8,12},{9,13},{1... | collective-permute-start | bytes 2359304 | tf_op jit(solution)/shard_map/ppermute | solution.py:174
  87.5 33.7 %copy-start.20 = (bf16[64,6144]{1,0:T(8,128)(2,1)}, bf16[64,6144]{1,0:T(8,128)(2,1)S(1)}, u32[]{:S(2)}) copy-start(bf16[64,6144]{1,0:T(8,128)(2,1)S(1)} %collective-permute-done.3.refs_4_) | copy-start | bytes 2359300
  87.5 17.8 %collective-permute-start.4 = (bf16[64,6144]{1,0:T(8,128)(2,1)S(1)}, bf16[64,6144]{1,0:T(8,128)(2,1)}, u32[]{:S(2)}, u32[]{:S(2)}) collective-permute-start(bf16[64,6144]{1,0:T(8,128)(2,1)S(1)} %collective-permute-done.3.refs_4_), channel_id=1, source_target_pairs={{0,1},{1,2},{2,3},{3,0},{4,5},{5,6},{6,7},{7,4},{8,9},{9,10},{10,1... | collective-permute-start | bytes 2359304 | tf_op jit(solution)/shard_map/ppermute | solution.py:174
  88.4 24.3 %collective-permute-start.25 = (bf16[64,6144]{1,0:T(8,128)(2,1)S(1)}, bf16[64,6144]{1,0:T(8,128)(2,1)S(1)}, u32[]{:S(2)}, u32[]{:S(2)}) collective-permute-start(bf16[64,6144]{1,0:T(8,128)(2,1)S(1)} %collective-permute-done.24.refs_4_), channel_id=1, source_target_pairs={{0,1},{1,2},{2,3},{3,0},{4,5},{5,6},{6,7},{7,4},{8,9},{9,10},{10,1... | collective-permute-start | bytes 2359304 | tf_op jit(solution)/shard_map/ppermute | solution.py:174
  95.9 17.8 %copy-start.18 = (bf16[64,6144]{1,0:T(8,128)(2,1)}, bf16[64,6144]{1,0:T(8,128)(2,1)S(1)}, u32[]{:S(2)}) copy-start(bf16[64,6144]{1,0:T(8,128)(2,1)S(1)} %collective-permute-done.12.refs_4_) | copy-start | bytes 2359300
  95.9 25.3 %collective-permute-start.13 = (bf16[64,6144]{1,0:T(8,128)(2,1)S(1)}, bf16[64,6144]{1,0:T(8,128)(2,1)S(1)}, u32[]{:S(2)}, u32[]{:S(2)}) collective-permute-start(bf16[64,6144]{1,0:T(8,128)(2,1)S(1)} %collective-permute-done.12.refs_4_), channel_id=1, source_target_pairs={{0,1},{1,2},{2,3},{3,0},{4,5},{5,6},{6,7},{7,4},{8,9},{9,10},{10,1... | collective-permute-start | bytes 2359304 | tf_op jit(solution)/shard_map/ppermute | solution.py:174
  96.8 26.5 %collective-permute-start.16 = (bf16[64,6144]{1,0:T(8,128)(2,1)}, bf16[64,6144]{1,0:T(8,128)(2,1)}, u32[]{:S(2)}, u32[]{:S(2)}) collective-permute-start(bf16[64,6144]{1,0:T(8,128)(2,1)} %collective-permute-done.15.refs_8_), channel_id=1, source_target_pairs={{0,4},{1,5},{2,6},{3,7},{4,8},{5,9},{6,10},{7,11},{8,12},{9,13},{1... | collective-permute-start | bytes 2359304 | tf_op jit(solution)/shard_map/ppermute | solution.py:174
  105.2 18.1 %collective-permute-start.11 = (bf16[64,6144]{1,0:T(8,128)(2,1)}, bf16[64,6144]{1,0:T(8,128)(2,1)}, u32[]{:S(2)}, u32[]{:S(2)}) collective-permute-start(bf16[64,6144]{1,0:T(8,128)(2,1)} %collective-permute-done.10.refs_9_), channel_id=1, source_target_pairs={{0,4},{1,5},{2,6},{3,7},{4,8},{5,9},{6,10},{7,11},{8,12},{9,13},{1... | collective-permute-start | bytes 2359304 | tf_op jit(solution)/shard_map/ppermute | solution.py:174
  105.3 24.4 %collective-permute-start.5 = (bf16[64,6144]{1,0:T(8,128)(2,1)}, bf16[64,6144]{1,0:T(8,128)(2,1)}, u32[]{:S(2)}, u32[]{:S(2)}) collective-permute-start(bf16[64,6144]{1,0:T(8,128)(2,1)} %collective-permute-done.4.refs_5_), channel_id=1, source_target_pairs={{0,1},{1,2},{2,3},{3,0},{4,5},{5,6},{6,7},{7,4},{8,9},{9,10},{10,1... | collective-permute-start | bytes 2359304 | tf_op jit(solution)/shard_map/ppermute | solution.py:174
  112.7 0.9 copy-start.16
  113.6 31.2 %collective-permute-start.19 = (bf16[64,6144]{1,0:T(8,128)(2,1)S(1)}, bf16[64,6144]{1,0:T(8,128)(2,1)}, u32[]{:S(2)}, u32[]{:S(2)}) collective-permute-start(bf16[64,6144]{1,0:T(8,128)(2,1)S(1)} %collective-permute-done.18.refs_4_), channel_id=1, source_target_pairs={{0,1},{1,2},{2,3},{3,0},{4,5},{5,6},{6,7},{7,4},{8,9},{9,10},{10,1... | collective-permute-start | bytes 2359304 | tf_op jit(solution)/shard_map/ppermute | solution.py:174
  121.2 0.9 copy-start.21
  122.1 22.8 %collective-permute-start.22 = (bf16[64,6144]{1,0:T(8,128)(2,1)}, bf16[64,6144]{1,0:T(8,128)(2,1)}, u32[]{:S(2)}, u32[]{:S(2)}) collective-permute-start(bf16[64,6144]{1,0:T(8,128)(2,1)} %collective-permute-done.21.refs_8_), channel_id=1, source_target_pairs={{0,4},{1,5},{2,6},{3,7},{4,8},{5,9},{6,10},{7,11},{8,12},{9,13},{1... | collective-permute-start | bytes 2359304 | tf_op jit(solution)/shard_map/ppermute | solution.py:174
  123.3 22.6 %collective-permute-start.28 = (bf16[64,6144]{1,0:T(8,128)(2,1)S(1)}, bf16[64,6144]{1,0:T(8,128)(2,1)}, u32[]{:S(2)}, u32[]{:S(2)}) collective-permute-start(bf16[64,6144]{1,0:T(8,128)(2,1)S(1)} %collective-permute-done.27.refs_8_), channel_id=1, source_target_pairs={{0,4},{1,5},{2,6},{3,7},{4,8},{5,9},{6,10},{7,11},{8,12},{9,13},{1... | collective-permute-start | bytes 2359304 | tf_op jit(solution)/shard_map/ppermute | solution.py:174
  123.3 23.5 %collective-permute-start.14 = (bf16[64,6144]{1,0:T(8,128)(2,1)}, bf16[64,6144]{1,0:T(8,128)(2,1)}, u32[]{:S(2)}, u32[]{:S(2)}) collective-permute-start(bf16[64,6144]{1,0:T(8,128)(2,1)} %copy-done.21), channel_id=1, source_target_pairs={{0,1},{1,2},{2,3},{3,0},{4,5},{5,6},{6,7},{7,4},{8,9},{9,10},{10,1... | collective-permute-start | bytes 2359304 | tf_op jit(solution)/shard_map/ppermute | solution.py:174
  129.7 22.7 %collective-permute-start.17 = (bf16[64,6144]{1,0:T(8,128)(2,1)}, bf16[64,6144]{1,0:T(8,128)(2,1)}, u32[]{:S(2)}, u32[]{:S(2)}) collective-permute-start(bf16[64,6144]{1,0:T(8,128)(2,1)} %collective-permute-done.16.refs_9_), channel_id=1, source_target_pairs={{0,4},{1,5},{2,6},{3,7},{4,8},{5,9},{6,10},{7,11},{8,12},{9,13},{1... | collective-permute-start | bytes 2359304 | tf_op jit(solution)/shard_map/ppermute | solution.py:174
  130.4 15.6 %copy-start.17 = (bf16[64,6144]{1,0:T(8,128)(2,1)S(1)}, bf16[64,6144]{1,0:T(8,128)(2,1)}, u32[]{:S(2)}) copy-start(bf16[64,6144]{1,0:T(8,128)(2,1)} %copy-done.16) | copy-start | bytes 2359300
  144.8 25.3 %collective-permute-start.20 = (bf16[64,6144]{1,0:T(8,128)(2,1)}, bf16[64,6144]{1,0:T(8,128)(2,1)S(1)}, u32[]{:S(2)}, u32[]{:S(2)}) collective-permute-start(bf16[64,6144]{1,0:T(8,128)(2,1)} %collective-permute-done.19.refs_5_), channel_id=1, source_target_pairs={{0,1},{1,2},{2,3},{3,0},{4,5},{5,6},{6,7},{7,4},{8,9},{9,10},{10,1... | collective-permute-start | bytes 2359304 | tf_op jit(solution)/shard_map/ppermute | solution.py:174
  144.9 25.3 %collective-permute-start.23 = (bf16[64,6144]{1,0:T(8,128)(2,1)}, bf16[64,6144]{1,0:T(8,128)(2,1)S(1)}, u32[]{:S(2)}, u32[]{:S(2)}) collective-permute-start(bf16[64,6144]{1,0:T(8,128)(2,1)} %collective-permute-done.22.refs_9_), channel_id=1, source_target_pairs={{0,4},{1,5},{2,6},{3,7},{4,8},{5,9},{6,10},{7,11},{8,12},{9,13},{1... | collective-permute-start | bytes 2359304 | tf_op jit(solution)/shard_map/ppermute | solution.py:174
  145.9 42.3 %collective-permute-start.26 = (bf16[64,6144]{1,0:T(8,128)(2,1)S(1)}, bf16[64,6144]{1,0:T(8,128)(2,1)S(1)}, u32[]{:S(2)}, u32[]{:S(2)}) collective-permute-start(bf16[64,6144]{1,0:T(8,128)(2,1)S(1)} %copy-done.17), channel_id=1, source_target_pairs={{0,1},{1,2},{2,3},{3,0},{4,5},{5,6},{6,7},{7,4},{8,9},{9,10},{10,1... | collective-permute-start | bytes 2359304 | tf_op jit(solution)/shard_map/ppermute | solution.py:174
  146.8 41.4 %collective-permute-start.29 = (bf16[64,6144]{1,0:T(8,128)(2,1)}, bf16[64,6144]{1,0:T(8,128)(2,1)S(1)}, u32[]{:S(2)}, u32[]{:S(2)}) collective-permute-start(bf16[64,6144]{1,0:T(8,128)(2,1)} %collective-permute-done.28.refs_9_), channel_id=1, source_target_pairs={{0,4},{1,5},{2,6},{3,7},{4,8},{5,9},{6,10},{7,11},{8,12},{9,13},{1... | collective-permute-start | bytes 2359304 | tf_op jit(solution)/shard_map/ppermute | solution.py:174
  170.2 0.9 copy-start.23
  171.0 0.9 copy-start.25
  188.2 18.3 %copy-start.10 = (bf16[2,256,256]{2,1,0:T(8,128)(2,1)S(1)}, bf16[2,256,256]{2,1,0:T(8,128)(2,1)}, u32[]{:S(2)}) copy-start(bf16[2,256,256]{2,1,0:T(8,128)(2,1)} %attend.4) | copy-start | bytes 786436
  188.2 18.3 %copy-start.11 = (bf16[2,256,256]{2,1,0:T(8,128)(2,1)S(1)}, bf16[2,256,256]{2,1,0:T(8,128)(2,1)}, u32[]{:S(2)}) copy-start(bf16[2,256,256]{2,1,0:T(8,128)(2,1)} %attend.5) | copy-start | bytes 786436
  188.2 18.3 %copy-start.12 = (bf16[2,256,256]{2,1,0:T(8,128)(2,1)S(1)}, bf16[2,256,256]{2,1,0:T(8,128)(2,1)}, u32[]{:S(2)}) copy-start(bf16[2,256,256]{2,1,0:T(8,128)(2,1)} %attend.6) | copy-start | bytes 786436
  188.2 0.9 copy-start.22
  189.1 0.9 copy-start.24
  206.6 1.0 copy-start.26
